TPU v7x, 32 devices: a whole 2x2x4 slice. The times are simulated.
32 devices in a mesh: row: 8 (over y, x, core), col: 4 (over z).
Axes of the slice: x: 2, y: 2, z: 4, core: 2. Of those that a mesh axis runs over, the one named last changes fastest.
Arguments:
- tiles: bfloat16 [8, 4, 128, 128, 128], P('row', 'col'), as said below
- coords: int32 [8, 4, 2, 128], P('row', 'col'), may hold values from 0 to 31, as said below
- counts: int32 [8, 4], P('row', 'col'), may hold values from 1 to 128, as said below
- valid: int32 [16384], P(('row', 'col')), may hold values 0 or 1
- start: float32 [8, 16384], P(None, ('row', 'col'))
- rotations: float32 [2, 8, 24], replicated, as said below
Outputs:
- eigenmaps: float32 [8, 16384], P(None, ('row', 'col'))
- ritz: float32 [8, 8], replicated
Inputs may be any that keep to these rules, and one draw needn't show every extreme that they name: coords[r, c, 0, s] is a block row from 0 to 15 and coords[r, c, 1, s] a block column from 0 to 31; the live slots of one owner name distinct blocks, each on or above the block diagonal (g_row <= g_col). The live slots of an owner are the first counts[r, c] of its list; one owner in grid row 0 has all 128 live. `tiles`: nonnegative; a tile on the block diagonal is symmetric. The Rayleigh-Ritz coefficients of the current vectors, rotations[t, :, 0 to 7], form a matrix whose diagonal dominates its rows.
All inputs are finite; a program needn't handle non-finite values. No bound on the sum of `valid` on one device may be relied on, other than what follows from the above.
Results may differ from a plain program's by a relative error of at most 0.0013.
Values may be sent and summed in bfloat16 or wider, within the bound.
A program may use at most 64 MiB of HBM per device.

v0:
```python
import functools
import jax
import jax.numpy as jnp
from jax import lax
from jax.experimental import pallas as pl
from jax.experimental.pallas import tpu as pltpu
from jax.sharding import PartitionSpec as P

F32 = jnp.float32
BF16 = jnp.bfloat16
MESH = pl.DeviceIdType.MESH
UNROLL = 8


def dot_high(left, right):
    return jnp.dot(left, right, precision=lax.Precision.HIGHEST, preferred_element_type=F32)


def dot_lanes(left, right, precision=None):
    return lax.dot_general(
        left, right, (((1,), (1,)), ((), ())), precision=precision, preferred_element_type=F32
    )


def split(values):
    high = values.astype(BF16)
    return high, (values - high.astype(F32)).astype(BF16)


def inverse_lower(gram):
    size = gram.shape[0]
    rows = lax.broadcasted_iota(jnp.int32, (size, size), 0)
    cols = lax.broadcasted_iota(jnp.int32, (size, size), 1)
    diag = rows == cols
    work = gram
    made = jnp.where(diag, 1.0, 0.0).astype(F32)
    for k in range(size - 1):
        column = work[:, k : k + 1]
        factor = jnp.where(rows[:, :1] > k, column / work[k : k + 1, k : k + 1], 0.0)
        work, made = work - factor * work[k : k + 1, :], made - factor * made[k : k + 1, :]
    pivots = jnp.sum(jnp.where(diag, work, 0.0), axis=1, keepdims=True)
    return made * lax.rsqrt(pivots)


def kernel(
    n_row, n_col, turns,
    tiles_hbm, places, places_vec, counts, valid, start, rotations,
    maps_out, ritz_out,
    tiles, pick_rows, pick_cols, direct, mirror, rows_total, cols_total,
    col_vecs, row_vecs, row_land, col_land, gram_row, gram_col,
    tile_sem, send_vec, recv_vec, send_sum, recv_sum, send_gram, recv_gram,
):
    me_row = lax.axis_index("row")
    me_col = lax.axis_index("col")
    slots, side, _ = tiles.shape
    count, stretch = start.shape
    per = stretch // side
    node_total = float(stretch * n_row * n_col)
    chunk = per * count

    fetch = pltpu.make_async_copy(tiles_hbm, tiles, tile_sem)
    fetch.start()

    def row_peer(d):
        return (lax.rem(me_row + d, n_row), me_col)

    def col_peer(d):
        return (me_row, lax.rem(me_col + d, n_col))

    peers = [("row", d) for d in range(1, n_row)] + [("col", d) for d in range(1, n_col)]
    barrier = pltpu.get_barrier_semaphore()
    for axis, d in peers:
        where = row_peer(d) if axis == "row" else col_peer(d)
        pl.semaphore_signal(barrier, inc=1, device_id=where, device_id_type=MESH)

    mask = valid[...].astype(F32)
    first = start[...] * mask

    def put_vectors(turn, top, bottom):
        both = jnp.concatenate([top, bottom], axis=0).astype(BF16)
        for k in range(per):
            part = both[:, k * side : (k + 1) * side]
            col_vecs[turn, me_row * per + k] = part
            row_vecs[turn, me_col * per + k] = part

    def vector_copies(turn):
        copies = []
        for at, (axis, d) in enumerate(peers):
            buffer, mine, where = (
                (col_vecs, me_row, row_peer(d)) if axis == "row" else (row_vecs, me_col, col_peer(d))
            )
            span = buffer.at[turn, pl.ds(mine * per, per)]
            copies.append(
                pltpu.make_async_remote_copy(
                    src_ref=span, dst_ref=span,
                    send_sem=send_vec.at[turn, at], recv_sem=recv_vec.at[turn, at],
                    device_id=where, device_id_type=MESH,
                )
            )
        return copies

    def sum_copies(turn, wide):
        copies = []
        height = chunk * (2 if wide else 1)
        for at, (axis, d) in enumerate(peers):
            total, land, there, where = (
                (cols_total, row_land, lax.rem(me_row + d, n_row), row_peer(d))
                if axis == "row"
                else (rows_total, col_land, lax.rem(me_col + d, n_col), col_peer(d))
            )
            copies.append(
                pltpu.make_async_remote_copy(
                    src_ref=total.at[turn, there, pl.ds(0, height)],
                    dst_ref=land.at[turn, d - 1, pl.ds(0, height)],
                    send_sem=send_sum.at[turn, at], recv_sem=recv_sum.at[turn, at],
                    device_id=where, device_id_type=MESH,
                )
            )
        return copies

    def gram_copies(turn, axis):
        copies = []
        for at, (name, d) in enumerate(peers):
            if name != axis:
                continue
            buffer, where = (gram_row, row_peer(d)) if axis == "row" else (gram_col, col_peer(d))
            copies.append(
                pltpu.make_async_remote_copy(
                    src_ref=buffer.at[turn, 0], dst_ref=buffer.at[turn, d],
                    send_sem=send_gram.at[turn, at], recv_sem=recv_gram.at[turn, at],
                    device_id=where, device_id_type=MESH,
                )
            )
        return copies

    started = []

    def begin(copies):
        for copy in copies:
            copy.start()
        started.extend(copies)
        return copies

    def arrive(copies):
        for copy in copies:
            copy.wait_recv()

    put_vectors(0, first, jnp.concatenate([mask, jnp.zeros((count - 1, stretch), F32)], axis=0))
    pl.semaphore_wait(barrier, len(peers))
    vec_moves = begin(vector_copies(0))

    spread = (
        lax.broadcasted_iota(jnp.int32, (slots, slots * count), 1) // count
        == lax.broadcasted_iota(jnp.int32, (slots, slots * count), 0)
    ).astype(F32).astype(BF16)
    at_rows = places_vec[0:1, :]
    at_cols = places_vec[1:2, :]
    slot_at = lax.broadcasted_iota(jnp.int32, (1, slots), 1)
    live = slot_at < counts[0, 0]
    whole_rows = me_row * (n_col * per) + at_rows
    whole_cols = (at_cols // per * n_col + me_col) * per + at_cols % per
    key_rows = jnp.where(live, at_rows, -1).astype(F32)
    key_cols = jnp.where(live & (whole_rows != whole_cols), at_cols, -1).astype(F32)
    keys = jnp.concatenate([key_rows, key_cols, jnp.zeros((14, slots), F32)], axis=0).astype(BF16)
    wide_keys = jnp.dot(keys, spread, preferred_element_type=F32)
    lane = (lax.broadcasted_iota(jnp.int32, (1, slots * count), 1) % count).astype(F32)
    for pick, wide_key in ((pick_rows, wide_keys[0:1]), (pick_cols, wide_keys[1:2])):
        wanted = wide_key * float(count) + lane
        for low in range(0, pick.shape[0], 64):
            row_at = (lax.broadcasted_iota(jnp.int32, (64, slots * count), 0) + low).astype(F32)
            pick[pl.ds(low, 64), :] = (row_at == wanted).astype(F32).astype(BF16)

    def local_product(turn, wide):
        def visit(step, carry):
            for more in range(UNROLL):
                slot = step * UNROLL + more
                tile = tiles[slot]
                by_col = col_vecs[turn, places[1, slot]]
                by_row = row_vecs[turn, places[0, slot]]
                forth = dot_lanes(by_col, tile)
                back = jnp.dot(by_row, tile, preferred_element_type=F32)
                at = pl.multiple_of(slot * count, count)
                if wide:
                    direct[0, pl.ds(at, count), :] = forth[:count]
                    direct[1, pl.ds(at, count), :] = forth[count:]
                    mirror[0, pl.ds(at, count), :] = back[:count]
                    mirror[1, pl.ds(at, count), :] = back[count:]
                else:
                    direct[0, pl.ds(at, count), :] = forth[:count] + forth[count:]
                    mirror[0, pl.ds(at, count), :] = back[:count] + back[count:]
            return carry

        lax.fori_loop(0, slots // UNROLL, visit, 0)
        for pick, terms, total, groups in (
            (pick_rows, direct, rows_total, n_col), (pick_cols, mirror, cols_total, n_row)
        ):
            for half in range(2 if wide else 1):
                high, low = split(terms[half])
                summed = jnp.dot(pick[...], high, preferred_element_type=F32)
                summed = summed + jnp.dot(pick[...], low, preferred_element_type=F32)
                for group in range(groups):
                    total[turn, group, pl.ds(half * chunk, chunk), :] = summed[
                        group * chunk : (group + 1) * chunk
                    ]

    def collect(turn, half):
        span = pl.ds(half * chunk, chunk)
        total = rows_total[turn, me_col, span, :] + cols_total[turn, me_row, span, :]
        for d in range(1, n_col):
            total = total + col_land[turn, d - 1, span, :]
        for d in range(1, n_row):
            total = total + row_land[turn, d - 1, span, :]
        return jnp.concatenate([total[k * count : (k + 1) * count] for k in range(per)], axis=1)

    def gram_begin(turn, vecs, images):
        both = jnp.concatenate([vecs, images], axis=0)
        gram_row[turn, 0] = jnp.zeros(gram_row.shape[2:], F32)
        gram_row[turn, 0, :, 0:count] = dot_lanes(both, vecs, lax.Precision.HIGHEST)
        return begin(gram_copies(turn, "row"))

    def gram_cross(turn, moves):
        arrive(moves)
        total = jnp.zeros(gram_row.shape[2:], F32)
        for r in range(n_row):
            total = total + gram_row[turn, lax.rem(me_row - r + n_row, n_row)]
        gram_col[turn, 0] = total
        return begin(gram_copies(turn, "col"))

    def gram_end(turn, moves):
        arrive(moves)
        total = jnp.zeros(gram_col.shape[2:], F32)
        for c in range(n_col):
            total = total + gram_col[turn, lax.rem(me_col - c + n_col, n_col)]
        total = total / node_total
        inverse = inverse_lower(total[:count, :count])
        theta = dot_lanes(dot_high(inverse, total[count:, :count]), inverse, lax.Precision.HIGHEST)
        return inverse, theta

    fetch.wait()
    arrive(vec_moves)
    local_product(0, True)
    arrive(begin(sum_copies(0, True)))
    product = collect(0, 0)
    degree = collect(0, 1)[0:1]
    vecs, images = first, mask * (degree * first - product)
    steps = step_images = None
    for turn in range(turns):
        high = images.astype(BF16).astype(F32)
        put_vectors(turn + 1, high, images - high)
        vec_moves = begin(vector_copies(turn + 1))
        gram_moves = gram_begin(turn, vecs, images)
        arrive(vec_moves)
        local_product(turn + 1, False)
        sum_moves = begin(sum_copies(turn + 1, False))
        gram_moves = gram_cross(turn, gram_moves)
        inverse, theta = gram_end(turn, gram_moves)
        parts = [vecs, images] + ([] if steps is None else [steps, step_images])
        settled = dot_high(inverse, jnp.concatenate(parts, axis=1))
        pair = settled[:, : 2 * stretch]
        turned = dot_high(theta, pair)
        resid = pair[:, stretch:] - turned[:, :stretch]
        rotation = rotations[turn]
        arrive(sum_moves)
        twice = mask * (degree * images - collect(turn + 1, 0))
        resid_images = dot_high(inverse, twice) - turned[:, stretch:]
        stack = [pair, jnp.concatenate([resid, resid_images], axis=1)]
        width = 2 * count
        if steps is not None:
            stack.append(settled[:, 2 * stretch :])
            width = 3 * count
        part = rotation[:, :width]
        lanes = lax.broadcasted_iota(jnp.int32, part.shape, 1)
        lead = jnp.concatenate([part, jnp.where(lanes < count, 0.0, part)], axis=0)
        moved = dot_high(lead, jnp.concatenate(stack, axis=0))
        vecs, images = moved[:count, :stretch], moved[:count, stretch:]
        steps, step_images = moved[count:, :stretch], moved[count:, stretch:]
    gram_moves = gram_begin(turns, vecs, images)
    inverse, theta = gram_end(turns, gram_cross(turns, gram_moves))
    maps_out[...] = dot_high(inverse, vecs)
    ritz_out[...] = theta
    for copy in started:
        copy.wait_send()


def body(tiles, coords, counts, valid, start, rotations):
    n_row = lax.axis_size("row")
    n_col = lax.axis_size("col")
    slots, side = tiles.shape[2], tiles.shape[3]
    count, stretch = start.shape
    per = stretch // side
    turns = rotations.shape[0]
    phases = turns + 1
    chunk = per * count
    links = n_row + n_col - 2
    vmem = pl.BlockSpec(memory_space=pltpu.VMEM)
    smem = pl.BlockSpec(memory_space=pltpu.SMEM)
    places = coords.reshape(2, slots)
    return pl.pallas_call(
        functools.partial(kernel, n_row, n_col, turns),
        out_shape=(
            jax.ShapeDtypeStruct((count, stretch), F32),
            jax.ShapeDtypeStruct((count, count), F32),
        ),
        in_specs=[pl.BlockSpec(memory_space=pl.ANY), smem, vmem, smem, vmem, vmem, vmem],
        out_specs=(vmem, vmem),
        scratch_shapes=[
            pltpu.VMEM((slots, side, side), BF16),
            pltpu.VMEM((n_col * chunk, slots * count), BF16),
            pltpu.VMEM((n_row * chunk, slots * count), BF16),
            pltpu.VMEM((2, slots * count, side), F32),
            pltpu.VMEM((2, slots * count, side), F32),
            pltpu.VMEM((phases, n_col, 2 * chunk, side), F32),
            pltpu.VMEM((phases, n_row, 2 * chunk, side), F32),
            pltpu.VMEM((phases, n_row * per, 2 * count, side), BF16),
            pltpu.VMEM((phases, n_col * per, 2 * count, side), BF16),
            pltpu.VMEM((phases, n_row - 1, 2 * chunk, side), F32),
            pltpu.VMEM((phases, n_col - 1, 2 * chunk, side), F32),
            pltpu.VMEM((phases, n_row, 2 * count, side), F32),
            pltpu.VMEM((phases, n_col, 2 * count, side), F32),
            pltpu.SemaphoreType.DMA(()),
        ]
        + [pltpu.SemaphoreType.DMA((phases, links))] * 6,
        compiler_params=pltpu.CompilerParams(
            collective_id=0, has_side_effects=True, vmem_limit_bytes=40 * 1024 * 1024
        ),
    )(
        tiles.reshape(slots, side, side), places, places, counts,
        valid.reshape(1, stretch), start, rotations,
    )


def solution(mesh):
    in_specs = (
        P("row", "col", None, None, None),
        P("row", "col", None, None),
        P("row", "col"),
        P(("row", "col")),
        P(None, ("row", "col")),
        P(),
    )
    out_specs = (P(None, ("row", "col")), P())
    return jax.shard_map(body, mesh=mesh, in_specs=in_specs, out_specs=out_specs, check_vma=False)
```

profile of v0, /device:TPU:0, one launch (start us, length us, event | category | flops | bytes accessed | tf_op | source)
XLA Modules:
  0.0 69.4 jit_solution(13094421181533813879)
XLA Ops:
  1.3 0.0 copy-start
  1.3 2.2 %copy-done = bf16[1,1,128,128,128]{4,3,2,1,0:T(8,128)(2,1)S(1)} copy-done((bf16[1,1,128,128,128]{4,3,2,1,0:T(8,128)(2,1)S(1)}, bf16[1,1,128,128,128]{4,3,2,1,0:T(8,128)(2,1)}, u32[]{:S(2)}) %copy-start) | copy-done | bytes 4194328
  3.5 0.0 copy-start.1
  3.5 0.7 %copy-done.1 = f32[8,512]{1,0:T(8,128)S(1)} copy-done((f32[8,512]{1,0:T(8,128)S(1)}, f32[8,512]{1,0:T(8,128)}, u32[]{:S(2)}) %copy-start.1) | copy-done | bytes 16408
  4.2 0.0 copy-start.2
  4.2 0.7 %copy-done.2 = f32[2,8,24]{2,1,0:T(8,128)S(1)} copy-done((f32[2,8,24]{2,1,0:T(8,128)S(1)}, f32[2,8,24]{2,1,0:T(8,128)}, u32[]{:S(2)}) %copy-start.2) | copy-done | bytes 1560
  4.9 0.0 copy-start.3
  4.9 0.7 copy-done.3
  5.6 0.0 copy-start.4
  5.6 0.7 copy-done.4
  6.2 61.9 %shard_map.77 = (f32[8,512]{1,0:T(8,128)S(1)}, f32[8,8]{1,0:T(8,128)S(1)}) custom-call(bf16[128,128,128]{2,1,0:T(8,128)(2,1)S(1)} %bitcast.3, s32[2,128]{1,0:T(2,128)S(1)} %bitcast.4, s32[2,128]{1,0:T(2,128)S(1)} %bitcast.5, s32[1,1]{1,0:T(1,128)S(6)} %copy.10.counts, s32[1,512]{1,0:T(1,128)S(1)} %bitcast.6, f32[8,512]{1,0:T(8,128)S(1)} %copy-done.1, ...), custom_call_target="tpu_custom_call" | custom-call | tf_op jit(solution)/shard_map/pallas_call | solution.py:298
  68.2 0.6 copy.11
  68.8 0.6 copy.12
Async XLA Ops:
  1.3 2.2 %copy-start = (bf16[1,1,128,128,128]{4,3,2,1,0:T(8,128)(2,1)S(1)}, bf16[1,1,128,128,128]{4,3,2,1,0:T(8,128)(2,1)}, u32[]{:S(2)}) copy-start(bf16[1,1,128,128,128]{4,3,2,1,0:T(8,128)(2,1)} %param.6) | copy-start | bytes 12582916
  3.5 0.7 %copy-start.1 = (f32[8,512]{1,0:T(8,128)S(1)}, f32[8,512]{1,0:T(8,128)}, u32[]{:S(2)}) copy-start(f32[8,512]{1,0:T(8,128)} %start.1) | copy-start | bytes 49156
  4.2 0.7 %copy-start.2 = (f32[2,8,24]{2,1,0:T(8,128)S(1)}, f32[2,8,24]{2,1,0:T(8,128)}, u32[]{:S(2)}) copy-start(f32[2,8,24]{2,1,0:T(8,128)} %rotations.1) | copy-start | bytes 4612
  4.9 0.7 copy-start.3
  5.6 0.7 copy-start.4
where the time goes:
time: 69.7 us; the launch traced here: 69.4 us
  Pallas kernels  61.9 us (89%)
  local copies, waits for them, and re-layouts  6.15 us (9%)
  between operations  1.3 us (2%)
    pallas_call x1, Pallas kernels, body(): pl.pallas_call(functools.partial(kernel, n_row, n_col, turns), out_shape=...  61.9 us
    unnamed x12, local copies, waits for them, and re-layouts  6.15 us

commit v1 on v0

--- a/solution.py
+++ b/solution.py
@@ -9,7 +9,7 @@
 F32 = jnp.float32
 BF16 = jnp.bfloat16
 MESH = pl.DeviceIdType.MESH
-UNROLL = 8
+UNROLL = 16
 
 
 def dot_high(left, right):
@@ -19,6 +19,20 @@
 def dot_lanes(left, right, precision=None):
     return lax.dot_general(
         left, right, (((1,), (1,)), ((), ())), precision=precision, preferred_element_type=F32
+    )
+
+
+def mix(left, right):
+    total = left[:, 0:1] * right[0:1, :]
+    for k in range(1, left.shape[1]):
+        total = total + left[:, k : k + 1] * right[k : k + 1, :]
+    return total
+
+
+def beside(first, second):
+    zero = jnp.zeros_like(first)
+    return jnp.concatenate(
+        [jnp.concatenate([first, zero], axis=1), jnp.concatenate([zero, second], axis=1)], axis=0
     )
 
 
@@ -101,7 +115,7 @@
 
     def sum_copies(turn, wide):
         copies = []
-        height = chunk * (2 if wide else 1)
+        height = chunk + (2 * count if wide else 0)
         for at, (axis, d) in enumerate(peers):
             total, land, there, where = (
                 (cols_total, row_land, lax.rem(me_row + d, n_row), row_peer(d))
@@ -172,45 +186,63 @@
 
     def local_product(turn, wide):
         def visit(step, carry):
-            for more in range(UNROLL):
+            for more in range(0, UNROLL, 2):
                 slot = step * UNROLL + more
-                tile = tiles[slot]
-                by_col = col_vecs[turn, places[1, slot]]
-                by_row = row_vecs[turn, places[0, slot]]
-                forth = dot_lanes(by_col, tile)
-                back = jnp.dot(by_row, tile, preferred_element_type=F32)
-                at = pl.multiple_of(slot * count, count)
-                if wide:
-                    direct[0, pl.ds(at, count), :] = forth[:count]
-                    direct[1, pl.ds(at, count), :] = forth[count:]
-                    mirror[0, pl.ds(at, count), :] = back[:count]
-                    mirror[1, pl.ds(at, count), :] = back[count:]
-                else:
-                    direct[0, pl.ds(at, count), :] = forth[:count] + forth[count:]
-                    mirror[0, pl.ds(at, count), :] = back[:count] + back[count:]
+                pair = tiles[pl.ds(slot, 2)].reshape(2 * side, side)
+                by_col = [col_vecs[turn, places[1, slot + i]] for i in range(2)]
+                by_row = [row_vecs[turn, places[0, slot + i]] for i in range(2)]
+                forth = dot_lanes(jnp.concatenate(by_col, axis=0), pair)
+                back = jnp.dot(beside(*by_row), pair, preferred_element_type=F32)
+                for i in range(2):
+                    at = pl.multiple_of((slot + i) * count, count)
+                    one = forth[2 * i * count : 2 * (i + 1) * count, i * side : (i + 1) * side]
+                    two = back[2 * i * count : 2 * (i + 1) * count]
+                    for terms, value in ((direct, one), (mirror, two)):
+                        if wide:
+                            terms[0, pl.ds(at, count), :] = value[:count]
+                            terms[1, pl.ds(at, count), :] = value[count:]
+                        else:
+                            terms[0, pl.ds(at, count), :] = value[:count] + value[count:]
             return carry
 
         lax.fori_loop(0, slots // UNROLL, visit, 0)
         for pick, terms, total, groups in (
-            (pick_rows, direct, rows_total, n_col), (pick_cols, mirror, cols_total, n_row)
+            (pick_cols, mirror, cols_total, n_row), (pick_rows, direct, rows_total, n_col)
         ):
             for half in range(2 if wide else 1):
                 high, low = split(terms[half])
                 summed = jnp.dot(pick[...], high, preferred_element_type=F32)
                 summed = summed + jnp.dot(pick[...], low, preferred_element_type=F32)
                 for group in range(groups):
-                    total[turn, group, pl.ds(half * chunk, chunk), :] = summed[
-                        group * chunk : (group + 1) * chunk
-                    ]
-
-    def collect(turn, half):
-        span = pl.ds(half * chunk, chunk)
-        total = rows_total[turn, me_col, span, :] + cols_total[turn, me_row, span, :]
+                    part = summed[group * chunk : (group + 1) * chunk]
+                    if half == 0:
+                        total[turn, group, pl.ds(0, chunk), :] = part.astype(BF16)
+                        continue
+                    rows = jnp.concatenate(
+                        [part[k * count : k * count + 1] for k in range(per)], axis=0
+                    )
+                    rest = rows - rows.astype(BF16).astype(F32)
+                    fill = jnp.zeros((2 * count - 2 * per, side), F32)
+                    rows = jnp.concatenate([rows, rest, fill], axis=0)
+                    total[turn, group, pl.ds(chunk, 2 * count), :] = rows.astype(BF16)
+
+    def gather_sums(turn, span):
+        total = rows_total[turn, me_col, span, :].astype(F32)
+        total = total + cols_total[turn, me_row, span, :].astype(F32)
         for d in range(1, n_col):
-            total = total + col_land[turn, d - 1, span, :]
+            total = total + col_land[turn, d - 1, span, :].astype(F32)
         for d in range(1, n_row):
-            total = total + row_land[turn, d - 1, span, :]
+            total = total + row_land[turn, d - 1, span, :].astype(F32)
+        return total
+
+    def collect(turn):
+        total = gather_sums(turn, pl.ds(0, chunk))
         return jnp.concatenate([total[k * count : (k + 1) * count] for k in range(per)], axis=1)
+
+    def collect_degree(turn):
+        total = gather_sums(turn, pl.ds(chunk, 2 * count))
+        total = total[:per] + total[per : 2 * per]
+        return jnp.concatenate([total[k : k + 1] for k in range(per)], axis=1)
 
     def gram_begin(turn, vecs, images):
         both = jnp.concatenate([vecs, images], axis=0)
@@ -240,9 +272,8 @@
     arrive(vec_moves)
     local_product(0, True)
     arrive(begin(sum_copies(0, True)))
-    product = collect(0, 0)
-    degree = collect(0, 1)[0:1]
-    vecs, images = first, mask * (degree * first - product)
+    degree = collect_degree(0)
+    vecs, images = first, mask * (degree * first - collect(0))
     steps = step_images = None
     for turn in range(turns):
         high = images.astype(BF16).astype(F32)
@@ -250,33 +281,31 @@
         vec_moves = begin(vector_copies(turn + 1))
         gram_moves = gram_begin(turn, vecs, images)
         arrive(vec_moves)
+        gram_moves = gram_cross(turn, gram_moves)
         local_product(turn + 1, False)
         sum_moves = begin(sum_copies(turn + 1, False))
-        gram_moves = gram_cross(turn, gram_moves)
         inverse, theta = gram_end(turn, gram_moves)
-        parts = [vecs, images] + ([] if steps is None else [steps, step_images])
-        settled = dot_high(inverse, jnp.concatenate(parts, axis=1))
-        pair = settled[:, : 2 * stretch]
-        turned = dot_high(theta, pair)
+        pair = mix(inverse, jnp.concatenate([vecs, images], axis=1))
+        turned = mix(theta, pair)
+        rotation = rotations[turn]
+        on_vecs, on_resid = rotation[:, :count], rotation[:, count : 2 * count]
         resid = pair[:, stretch:] - turned[:, :stretch]
-        rotation = rotations[turn]
+        moved = mix(on_resid, jnp.concatenate([resid, -turned[:, stretch:]], axis=1))
+        if steps is not None:
+            old = mix(inverse, jnp.concatenate([steps, step_images], axis=1))
+            moved = moved + mix(rotation[:, 2 * count :], old)
+        kept = mix(on_vecs, pair)
+        on_twice = mix(on_resid, inverse)
+        steps = moved[:, :stretch]
+        vecs = kept[:, :stretch] + steps
+        scaled = degree * images
         arrive(sum_moves)
-        twice = mask * (degree * images - collect(turn + 1, 0))
-        resid_images = dot_high(inverse, twice) - turned[:, stretch:]
-        stack = [pair, jnp.concatenate([resid, resid_images], axis=1)]
-        width = 2 * count
-        if steps is not None:
-            stack.append(settled[:, 2 * stretch :])
-            width = 3 * count
-        part = rotation[:, :width]
-        lanes = lax.broadcasted_iota(jnp.int32, part.shape, 1)
-        lead = jnp.concatenate([part, jnp.where(lanes < count, 0.0, part)], axis=0)
-        moved = dot_high(lead, jnp.concatenate(stack, axis=0))
-        vecs, images = moved[:count, :stretch], moved[:count, stretch:]
-        steps, step_images = moved[count:, :stretch], moved[count:, stretch:]
+        twice = mask * (scaled - collect(turn + 1))
+        step_images = moved[:, stretch:] + mix(on_twice, twice)
+        images = kept[:, stretch:] + step_images
     gram_moves = gram_begin(turns, vecs, images)
     inverse, theta = gram_end(turns, gram_cross(turns, gram_moves))
-    maps_out[...] = dot_high(inverse, vecs)
+    maps_out[...] = mix(inverse, vecs)
     ritz_out[...] = theta
     for copy in started:
         copy.wait_send()
@@ -309,19 +338,19 @@
             pltpu.VMEM((n_row * chunk, slots * count), BF16),
             pltpu.VMEM((2, slots * count, side), F32),
             pltpu.VMEM((2, slots * count, side), F32),
-            pltpu.VMEM((phases, n_col, 2 * chunk, side), F32),
-            pltpu.VMEM((phases, n_row, 2 * chunk, side), F32),
+            pltpu.VMEM((phases, n_col, chunk + 2 * count, side), BF16),
+            pltpu.VMEM((phases, n_row, chunk + 2 * count, side), BF16),
             pltpu.VMEM((phases, n_row * per, 2 * count, side), BF16),
             pltpu.VMEM((phases, n_col * per, 2 * count, side), BF16),
-            pltpu.VMEM((phases, n_row - 1, 2 * chunk, side), F32),
-            pltpu.VMEM((phases, n_col - 1, 2 * chunk, side), F32),
+            pltpu.VMEM((phases, n_row - 1, chunk + 2 * count, side), BF16),
+            pltpu.VMEM((phases, n_col - 1, chunk + 2 * count, side), BF16),
             pltpu.VMEM((phases, n_row, 2 * count, side), F32),
             pltpu.VMEM((phases, n_col, 2 * count, side), F32),
             pltpu.SemaphoreType.DMA(()),
         ]
         + [pltpu.SemaphoreType.DMA((phases, links))] * 6,
         compiler_params=pltpu.CompilerParams(
-            collective_id=0, has_side_effects=True, vmem_limit_bytes=40 * 1024 * 1024
+            collective_id=0, has_side_effects=True, vmem_limit_bytes=60 * 1024 * 1024
         ),
     )(
         tiles.reshape(slots, side, side), places, places, counts,

time: 69.7 us -> 54.1 us (0.78)
  Pallas kernels: 61.9 us -> 50 us
  local copies, waits for them, and re-layouts: 6.15 us -> 2.59 us
    pallas_call x1, Pallas kernels: 61.9 us -> 50 us  [body(): pl.pallas_call(functools.partial(kernel, n_row, n_col, turns), out_shape=...]
    unnamed x12 -> x2, local copies, waits for them, and re-layouts: 6.15 us -> 2.59 us
where the time goes in v1:
time: 54.1 us; the launch traced here: 53.8 us
  Pallas kernels  50 us (92%)
  local copies, waits for them, and re-layouts  2.59 us (5%)
  between operations  1.28 us (2%)
    pallas_call x1, Pallas kernels, body(): pl.pallas_call(functools.partial(kernel, n_row, n_col, turns), out_shape=...  50 us
    unnamed x2, local copies, waits for them, and re-layouts  2.59 us

profile of v1, /device:TPU:0, one launch (start us, length us, event | category | flops | bytes accessed | tf_op | source)
XLA Modules:
  0.0 53.8 jit_solution(14070874501877267426)
XLA Ops:
  1.3 50.0 %shard_map.77 = (f32[8,512]{1,0:T(8,128)}, f32[8,8]{1,0:T(8,128)}) custom-call(bf16[128,128,128]{2,1,0:T(8,128)(2,1)} %bitcast.3, s32[2,128]{1,0:T(2,128)} %bitcast.4, s32[2,128]{1,0:T(2,128)} %bitcast.5, s32[1,1]{1,0:T(1,128)S(6)} %copy.10.counts, s32[1,512]{1,0:T(1,128)} %bitcast.6, f32[8,512]{1,0:T(8,128)} %start.1, f32[2,8,24]{2,1,0:T(8,128)} %rotations.1), custom_call_target="tpu_custom_call" | custom-call | tf_op jit(solution)/shard_map/pallas_call | solution.py:327
  51.2 1.3 %copy.11 = f32[8,512]{1,0:T(8,128)} copy(f32[8,512]{1,0:T(8,128)} %get-tuple-element.4) | data formatting | bytes 32768
  52.6 1.3 %copy.12 = f32[8,8]{1,0:T(8,128)} copy(f32[8,8]{1,0:T(8,128)} %get-tuple-element.5) | data formatting | bytes 512

commit v2 on v1

--- a/solution.py
+++ b/solution.py
@@ -60,7 +60,7 @@
     n_row, n_col, turns,
     tiles_hbm, places, places_vec, counts, valid, start, rotations,
     maps_out, ritz_out,
-    tiles, pick_rows, pick_cols, direct, mirror, rows_total, cols_total,
+    tiles, pick_rows, pick_cols, pick_half, direct, mirror, rows_total, cols_total,
     col_vecs, row_vecs, row_land, col_land, gram_row, gram_col,
     tile_sem, send_vec, recv_vec, send_sum, recv_sum, send_gram, recv_gram,
 ):
@@ -175,7 +175,9 @@
     whole_cols = (at_cols // per * n_col + me_col) * per + at_cols % per
     key_rows = jnp.where(live, at_rows, -1).astype(F32)
     key_cols = jnp.where(live & (whole_rows != whole_cols), at_cols, -1).astype(F32)
-    keys = jnp.concatenate([key_rows, key_cols, jnp.zeros((14, slots), F32)], axis=0).astype(BF16)
+    weights = jnp.where(whole_rows != whole_cols, 1.0, 0.5).astype(F32)
+    keys = [key_rows, key_cols, weights, jnp.zeros((13, slots), F32)]
+    keys = jnp.concatenate(keys, axis=0).astype(BF16)
     wide_keys = jnp.dot(keys, spread, preferred_element_type=F32)
     lane = (lax.broadcasted_iota(jnp.int32, (1, slots * count), 1) % count).astype(F32)
     for pick, wide_key in ((pick_rows, wide_keys[0:1]), (pick_cols, wide_keys[1:2])):
@@ -183,6 +185,39 @@
         for low in range(0, pick.shape[0], 64):
             row_at = (lax.broadcasted_iota(jnp.int32, (64, slots * count), 0) + low).astype(F32)
             pick[pl.ds(low, 64), :] = (row_at == wanted).astype(F32).astype(BF16)
+
+    def build_half():
+        wanted = wide_keys[0:1] * float(count) + lane
+        for low in range(0, pick_half.shape[0], 64):
+            row_at = (lax.broadcasted_iota(jnp.int32, (64, slots * count), 0) + low).astype(F32)
+            pick_half[pl.ds(low, 64), :] = jnp.where(row_at == wanted, wide_keys[2:3], 0.0).astype(BF16)
+
+    def local_form(turn, vecs, scaled):
+        def visit(step, carry):
+            for more in range(0, UNROLL, 2):
+                slot = step * UNROLL + more
+                pair = tiles[pl.ds(slot, 2)].reshape(2 * side, side)
+                by_col = [col_vecs[turn, places[1, slot + i]] for i in range(2)]
+                forth = dot_lanes(jnp.concatenate(by_col, axis=0), pair)
+                for i in range(2):
+                    at = pl.multiple_of((slot + i) * count, count)
+                    value = forth[2 * i * count : 2 * (i + 1) * count, i * side : (i + 1) * side]
+                    direct[0, pl.ds(at, count), :] = value[:count] + value[count:]
+            return carry
+
+        lax.fori_loop(0, slots // UNROLL, visit, 0)
+        high, low = split(direct[0])
+        summed = jnp.dot(pick_half[...], high, preferred_element_type=F32)
+        summed = summed + jnp.dot(pick_half[...], low, preferred_element_type=F32)
+        blocks = summed.shape[0] // count
+        left = [summed[p * count : (p + 1) * count] for p in range(blocks)]
+        right = [row_vecs[turn, p].astype(F32) for p in range(blocks)]
+        right = [value[:count] + value[count:] for value in right]
+        left = jnp.concatenate(left + [-0.5 * scaled], axis=1)
+        right = jnp.concatenate(right + [vecs], axis=1)
+        both = jnp.concatenate([left, right], axis=0)
+        cross = dot_lanes(both, both, lax.Precision.HIGHEST)
+        return -(cross[:count, count:] + cross[count:, :count])
 
     def local_product(turn, wide):
         def visit(step, carry):
@@ -244,11 +279,14 @@
         total = total[:per] + total[per : 2 * per]
         return jnp.concatenate([total[k : k + 1] for k in range(per)], axis=1)
 
+    def gram_send(turn, grams):
+        gram_row[turn, 0] = jnp.zeros(gram_row.shape[2:], F32)
+        gram_row[turn, 0, :, 0:count] = grams
+        return begin(gram_copies(turn, "row"))
+
     def gram_begin(turn, vecs, images):
         both = jnp.concatenate([vecs, images], axis=0)
-        gram_row[turn, 0] = jnp.zeros(gram_row.shape[2:], F32)
-        gram_row[turn, 0, :, 0:count] = dot_lanes(both, vecs, lax.Precision.HIGHEST)
-        return begin(gram_copies(turn, "row"))
+        return gram_send(turn, dot_lanes(both, vecs, lax.Precision.HIGHEST))
 
     def gram_cross(turn, moves):
         arrive(moves)
@@ -271,7 +309,9 @@
     fetch.wait()
     arrive(vec_moves)
     local_product(0, True)
-    arrive(begin(sum_copies(0, True)))
+    sum_moves = begin(sum_copies(0, True))
+    build_half()
+    arrive(sum_moves)
     degree = collect_degree(0)
     vecs, images = first, mask * (degree * first - collect(0))
     steps = step_images = None
@@ -282,8 +322,13 @@
         gram_moves = gram_begin(turn, vecs, images)
         arrive(vec_moves)
         gram_moves = gram_cross(turn, gram_moves)
-        local_product(turn + 1, False)
-        sum_moves = begin(sum_copies(turn + 1, False))
+        last = turn == turns - 1
+        scaled = degree * images
+        if last:
+            form = local_form(turn + 1, images, mask * scaled)
+        else:
+            local_product(turn + 1, False)
+            sum_moves = begin(sum_copies(turn + 1, False))
         inverse, theta = gram_end(turn, gram_moves)
         pair = mix(inverse, jnp.concatenate([vecs, images], axis=1))
         turned = mix(theta, pair)
@@ -298,12 +343,20 @@
         on_twice = mix(on_resid, inverse)
         steps = moved[:, :stretch]
         vecs = kept[:, :stretch] + steps
-        scaled = degree * images
+        if last:
+            rest = moved[:, stretch:] + kept[:, stretch:]
+            sides = jnp.concatenate([vecs, rest], axis=0)
+            stack = jnp.concatenate([sides, mix(on_twice, images)], axis=0)
+            known = dot_lanes(stack, sides, lax.Precision.HIGHEST)
+            gram_x = known[:count, :count]
+            gram_ax = known[count : 2 * count, :count] + known[2 * count :, count:]
+            gram_ax = gram_ax + dot_lanes(mix(on_twice, form), on_twice, lax.Precision.HIGHEST)
+            break
         arrive(sum_moves)
         twice = mask * (scaled - collect(turn + 1))
         step_images = moved[:, stretch:] + mix(on_twice, twice)
         images = kept[:, stretch:] + step_images
-    gram_moves = gram_begin(turns, vecs, images)
+    gram_moves = gram_send(turns, jnp.concatenate([gram_x, gram_ax], axis=0))
     inverse, theta = gram_end(turns, gram_cross(turns, gram_moves))
     maps_out[...] = mix(inverse, vecs)
     ritz_out[...] = theta
@@ -336,19 +389,22 @@
             pltpu.VMEM((slots, side, side), BF16),
             pltpu.VMEM((n_col * chunk, slots * count), BF16),
             pltpu.VMEM((n_row * chunk, slots * count), BF16),
+            pltpu.VMEM((n_col * chunk, slots * count), BF16),
             pltpu.VMEM((2, slots * count, side), F32),
             pltpu.VMEM((2, slots * count, side), F32),
-            pltpu.VMEM((phases, n_col, chunk + 2 * count, side), BF16),
-            pltpu.VMEM((phases, n_row, chunk + 2 * count, side), BF16),
+            pltpu.VMEM((turns, n_col, chunk + 2 * count, side), BF16),
+            pltpu.VMEM((turns, n_row, chunk + 2 * count, side), BF16),
             pltpu.VMEM((phases, n_row * per, 2 * count, side), BF16),
             pltpu.VMEM((phases, n_col * per, 2 * count, side), BF16),
-            pltpu.VMEM((phases, n_row - 1, chunk + 2 * count, side), BF16),
-            pltpu.VMEM((phases, n_col - 1, chunk + 2 * count, side), BF16),
+            pltpu.VMEM((turns, n_row - 1, chunk + 2 * count, side), BF16),
+            pltpu.VMEM((turns, n_col - 1, chunk + 2 * count, side), BF16),
             pltpu.VMEM((phases, n_row, 2 * count, side), F32),
             pltpu.VMEM((phases, n_col, 2 * count, side), F32),
             pltpu.SemaphoreType.DMA(()),
         ]
-        + [pltpu.SemaphoreType.DMA((phases, links))] * 6,
+        + [pltpu.SemaphoreType.DMA((phases, links))] * 2
+        + [pltpu.SemaphoreType.DMA((turns, links))] * 2
+        + [pltpu.SemaphoreType.DMA((phases, links))] * 2,
         compiler_params=pltpu.CompilerParams(
             collective_id=0, has_side_effects=True, vmem_limit_bytes=60 * 1024 * 1024
         ),

time: 54.1 us -> 51.9 us (0.959)
  Pallas kernels: 50 us -> 47.7 us
    pallas_call x1, Pallas kernels: 50 us -> 47.7 us  [body(): pl.pallas_call(functools.partial(kernel, n_row, n_col, turns), out_shape=...]
where the time goes in v2:
time: 51.9 us; the launch traced here: 51.6 us
  Pallas kernels  47.7 us (92%)
  local copies, waits for them, and re-layouts  2.59 us (5%)
  between operations  1.28 us (2%)
    pallas_call x1, Pallas kernels, body(): pl.pallas_call(functools.partial(kernel, n_row, n_col, turns), out_shape=...  47.7 us
    unnamed x2, local copies, waits for them, and re-layouts  2.59 us

profile of v2, /device:TPU:0, one launch (start us, length us, event | category | flops | bytes accessed | tf_op | source)
XLA Modules:
  0.0 51.6 jit_solution(120263836609033032)
XLA Ops:
  1.3 47.7 %shard_map.77 = (f32[8,512]{1,0:T(8,128)}, f32[8,8]{1,0:T(8,128)}) custom-call(bf16[128,128,128]{2,1,0:T(8,128)(2,1)} %bitcast.3, s32[2,128]{1,0:T(2,128)} %bitcast.4, s32[2,128]{1,0:T(2,128)} %bitcast.5, s32[1,1]{1,0:T(1,128)S(6)} %copy.10.counts, s32[1,512]{1,0:T(1,128)} %bitcast.6, f32[8,512]{1,0:T(8,128)} %start.1, f32[2,8,24]{2,1,0:T(8,128)} %rotations.1), custom_call_target="tpu_custom_call" | custom-call | tf_op jit(solution)/shard_map/pallas_call | solution.py:380
  49.0 1.3 %copy.11 = f32[8,512]{1,0:T(8,128)} copy(f32[8,512]{1,0:T(8,128)} %get-tuple-element.4) | data formatting | bytes 32768
  50.3 1.3 %copy.12 = f32[8,8]{1,0:T(8,128)} copy(f32[8,8]{1,0:T(8,128)} %get-tuple-element.5) | data formatting | bytes 512

commit v3 on v2

--- a/solution.py
+++ b/solution.py
@@ -9,7 +9,7 @@
 F32 = jnp.float32
 BF16 = jnp.bfloat16
 MESH = pl.DeviceIdType.MESH
-UNROLL = 16
+UNROLL = 64
 
 
 def dot_high(left, right):
@@ -364,6 +364,11 @@
         copy.wait_send()
 
 
+def hand_out(maps_in, ritz_in, maps_out, ritz_out):
+    maps_out[...] = maps_in[...]
+    ritz_out[...] = ritz_in[...]
+
+
 def body(tiles, coords, counts, valid, start, rotations):
     n_row = lax.axis_size("row")
     n_col = lax.axis_size("col")
@@ -377,7 +382,7 @@
     vmem = pl.BlockSpec(memory_space=pltpu.VMEM)
     smem = pl.BlockSpec(memory_space=pltpu.SMEM)
     places = coords.reshape(2, slots)
-    return pl.pallas_call(
+    results = pl.pallas_call(
         functools.partial(kernel, n_row, n_col, turns),
         out_shape=(
             jax.ShapeDtypeStruct((count, stretch), F32),
@@ -412,6 +417,12 @@
         tiles.reshape(slots, side, side), places, places, counts,
         valid.reshape(1, stretch), start, rotations,
     )
+    return pl.pallas_call(
+        hand_out,
+        out_shape=tuple(jax.ShapeDtypeStruct(part.shape, part.dtype) for part in results),
+        in_specs=[vmem, vmem],
+        out_specs=(vmem, vmem),
+    )(*results)
 
 
 def solution(mesh):

time: 51.9 us -> 48.9 us (0.942)
  local copies, waits for them, and re-layouts: 2.59 us -> 0 us
    unnamed x2 -> x0, local copies, waits for them, and re-layouts: 2.59 us -> none
    pallas_call x1, Pallas kernels: 47.7 us -> 46 us  [body(): pl.pallas_call(functools.partial(kernel, n_row, n_col, turns), out_shape=...]
    pallas_call x0 -> x1, Pallas kernels: none -> 1.33 us  [body(): pl.pallas_call(hand_out, out_shape=tuple((jax.ShapeDtypeStruct(part.shape...]
where the time goes in v3:
time: 48.9 us; the launch traced here: 48.6 us
  Pallas kernels  47.4 us (97%)
  between operations  1.28 us (3%)
    pallas_call x1, Pallas kernels, body(): pl.pallas_call(functools.partial(kernel, n_row, n_col, turns), out_shape=...  46 us
    pallas_call x1, Pallas kernels, body(): pl.pallas_call(hand_out, out_shape=tuple((jax.ShapeDtypeStruct(part.shape...  1.33 us

profile of v3, /device:TPU:0, one launch (start us, length us, event | category | flops | bytes accessed | tf_op | source)
XLA Modules:
  0.0 48.6 jit_solution(14422047216775222614)
XLA Ops:
  1.3 46.0 %shard_map.77 = (f32[8,512]{1,0:T(8,128)}, f32[8,8]{1,0:T(8,128)}) custom-call(bf16[128,128,128]{2,1,0:T(8,128)(2,1)} %bitcast.3, s32[2,128]{1,0:T(2,128)} %bitcast.4, s32[2,128]{1,0:T(2,128)} %bitcast.5, s32[1,1]{1,0:T(1,128)S(6)} %copy.8.counts, s32[1,512]{1,0:T(1,128)} %bitcast.6, f32[8,512]{1,0:T(8,128)} %start.1, f32[2,8,24]{2,1,0:T(8,128)} %rotations.1), custom_call_target="tpu_custom_call" | custom-call | tf_op jit(solution)/shard_map/pallas_call | solution.py:385
  47.3 1.3 %shard_map.78 = (f32[8,512]{1,0:T(8,128)}, f32[8,8]{1,0:T(8,128)}) custom-call(f32[8,512]{1,0:T(8,128)} %get-tuple-element.4.maps_in, f32[8,8]{1,0:T(8,128)} %get-tuple-element.5.ritz_in), custom_call_target="tpu_custom_call" | custom-call | tf_op jit(solution)/shard_map/pallas_call | solution.py:420

commit v4 on v3

--- a/solution.py
+++ b/solution.py
@@ -281,7 +281,7 @@
 
     def gram_send(turn, grams):
         gram_row[turn, 0] = jnp.zeros(gram_row.shape[2:], F32)
-        gram_row[turn, 0, :, 0:count] = grams
+        gram_row[turn, 0, 0 : grams.shape[0], 0 : grams.shape[1]] = grams
         return begin(gram_copies(turn, "row"))
 
     def gram_begin(turn, vecs, images):
@@ -301,10 +301,14 @@
         total = jnp.zeros(gram_col.shape[2:], F32)
         for c in range(n_col):
             total = total + gram_col[turn, lax.rem(me_col - c + n_col, n_col)]
-        total = total / node_total
+        return total / node_total
+
+    def congruence(left, inner):
+        return dot_lanes(dot_high(left, inner), left, lax.Precision.HIGHEST)
+
+    def settle_small(total):
         inverse = inverse_lower(total[:count, :count])
-        theta = dot_lanes(dot_high(inverse, total[count:, :count]), inverse, lax.Precision.HIGHEST)
-        return inverse, theta
+        return inverse, congruence(inverse, total[count : 2 * count, :count])
 
     fetch.wait()
     arrive(vec_moves)
@@ -319,17 +323,21 @@
         high = images.astype(BF16).astype(F32)
         put_vectors(turn + 1, high, images - high)
         vec_moves = begin(vector_copies(turn + 1))
+        last = turn == turns - 1
+        scaled = degree * images
+        if last:
+            basis = jnp.concatenate([vecs, images, steps, step_images], axis=0)
+            gram_moves = gram_send(turn, dot_lanes(basis, basis, lax.Precision.HIGHEST))
+            arrive(vec_moves)
+            gram_moves = gram_cross(turn, gram_moves)
+            form = local_form(turn + 1, images, mask * scaled)
+            break
         gram_moves = gram_begin(turn, vecs, images)
         arrive(vec_moves)
         gram_moves = gram_cross(turn, gram_moves)
-        last = turn == turns - 1
-        scaled = degree * images
-        if last:
-            form = local_form(turn + 1, images, mask * scaled)
-        else:
-            local_product(turn + 1, False)
-            sum_moves = begin(sum_copies(turn + 1, False))
-        inverse, theta = gram_end(turn, gram_moves)
+        local_product(turn + 1, False)
+        sum_moves = begin(sum_copies(turn + 1, False))
+        inverse, theta = settle_small(gram_end(turn, gram_moves))
         pair = mix(inverse, jnp.concatenate([vecs, images], axis=1))
         turned = mix(theta, pair)
         rotation = rotations[turn]
@@ -343,23 +351,32 @@
         on_twice = mix(on_resid, inverse)
         steps = moved[:, :stretch]
         vecs = kept[:, :stretch] + steps
-        if last:
-            rest = moved[:, stretch:] + kept[:, stretch:]
-            sides = jnp.concatenate([vecs, rest], axis=0)
-            stack = jnp.concatenate([sides, mix(on_twice, images)], axis=0)
-            known = dot_lanes(stack, sides, lax.Precision.HIGHEST)
-            gram_x = known[:count, :count]
-            gram_ax = known[count : 2 * count, :count] + known[2 * count :, count:]
-            gram_ax = gram_ax + dot_lanes(mix(on_twice, form), on_twice, lax.Precision.HIGHEST)
-            break
         arrive(sum_moves)
         twice = mask * (scaled - collect(turn + 1))
         step_images = moved[:, stretch:] + mix(on_twice, twice)
         images = kept[:, stretch:] + step_images
-    gram_moves = gram_send(turns, jnp.concatenate([gram_x, gram_ax], axis=0))
-    inverse, theta = gram_end(turns, gram_cross(turns, gram_moves))
-    maps_out[...] = mix(inverse, vecs)
-    ritz_out[...] = theta
+    form_moves = gram_send(turns, form)
+    total = gram_end(turns - 1, gram_moves)[:, : 4 * count]
+    inverse, theta = settle_small(total)
+    rotation = rotations[turns - 1]
+    on_vecs, on_resid = rotation[:, :count], rotation[:, count : 2 * count]
+    on_resid, on_steps = mix(on_resid, inverse), mix(rotation[:, 2 * count :], inverse)
+    on_vecs = mix(on_vecs - mix(rotation[:, count : 2 * count], theta), inverse)
+    zero = jnp.zeros_like(inverse)
+    on_basis = jnp.concatenate([on_vecs, on_resid, on_steps, zero], axis=1)
+    on_rest = jnp.concatenate([zero, on_vecs, zero, on_steps], axis=1)
+    form_moves = gram_cross(turns, form_moves)
+    sides = dot_high(jnp.concatenate([on_basis, on_rest], axis=0), total)
+    sides = dot_lanes(sides, on_basis, lax.Precision.HIGHEST)
+    crossed = mix(on_resid, total[count : 2 * count])
+    known = sides[count:] + dot_lanes(crossed, on_rest, lax.Precision.HIGHEST)
+    inverse = inverse_lower(sides[:count])
+    known = congruence(inverse, known)
+    outer = mix(inverse, on_resid)
+    maps = mix(on_vecs, vecs) + mix(on_resid, images) + mix(on_steps, steps)
+    maps_out[...] = mix(inverse, maps)
+    form = gram_end(turns, form_moves)[:count, :count]
+    ritz_out[...] = known + congruence(outer, form)
     for copy in started:
         copy.wait_send()
 
@@ -403,8 +420,8 @@
             pltpu.VMEM((phases, n_col * per, 2 * count, side), BF16),
             pltpu.VMEM((turns, n_row - 1, chunk + 2 * count, side), BF16),
             pltpu.VMEM((turns, n_col - 1, chunk + 2 * count, side), BF16),
-            pltpu.VMEM((phases, n_row, 2 * count, side), F32),
-            pltpu.VMEM((phases, n_col, 2 * count, side), F32),
+            pltpu.VMEM((phases, n_row, 4 * count, side), F32),
+            pltpu.VMEM((phases, n_col, 4 * count, side), F32),
             pltpu.SemaphoreType.DMA(()),
         ]
         + [pltpu.SemaphoreType.DMA((phases, links))] * 2

time: 48.9 us -> 48.9 us (level)
  no operation moved by 1% of the time
where the time goes in v4:
time: 48.9 us; the launch traced here: 48.6 us
  Pallas kernels  47.3 us (97%)
  between operations  1.28 us (3%)
    pallas_call x1, Pallas kernels, body(): pl.pallas_call(functools.partial(kernel, n_row, n_col, turns), out_shape=...  46 us
    pallas_call x1, Pallas kernels, body(): pl.pallas_call(hand_out, out_shape=tuple((jax.ShapeDtypeStruct(part.shape...  1.33 us

profile of v4, /device:TPU:0, one launch (start us, length us, event | category | flops | bytes accessed | tf_op | source)
XLA Modules:
  0.0 48.6 jit_solution(8447578533295979876)
XLA Ops:
  1.3 46.0 %shard_map.77 = (f32[8,512]{1,0:T(8,128)}, f32[8,8]{1,0:T(8,128)}) custom-call(bf16[128,128,128]{2,1,0:T(8,128)(2,1)} %bitcast.3, s32[2,128]{1,0:T(2,128)} %bitcast.4, s32[2,128]{1,0:T(2,128)} %bitcast.5, s32[1,1]{1,0:T(1,128)S(6)} %copy.8.counts, s32[1,512]{1,0:T(1,128)} %bitcast.6, f32[8,512]{1,0:T(8,128)} %start.1, f32[2,8,24]{2,1,0:T(8,128)} %rotations.1), custom_call_target="tpu_custom_call" | custom-call | tf_op jit(solution)/shard_map/pallas_call | solution.py:402
  47.2 1.3 %shard_map.78 = (f32[8,512]{1,0:T(8,128)}, f32[8,8]{1,0:T(8,128)}) custom-call(f32[8,512]{1,0:T(8,128)} %get-tuple-element.4.maps_in, f32[8,8]{1,0:T(8,128)} %get-tuple-element.5.ritz_in), custom_call_target="tpu_custom_call" | custom-call | tf_op jit(solution)/shard_map/pallas_call | solution.py:437
